TPU v7x, 32 devices: a whole 2x2x4 slice. The times are simulated.
32 devices in a mesh: row: 8 (over y, x, core), col: 4 (over z).
Axes of the slice: x: 2, y: 2, z: 4, core: 2. Of those that a mesh axis runs over, the one named last changes fastest.
Arguments:
- u_factors: bfloat16 [24, 24, 1024, 128], P('row', 'col'), may hold values from -0.109375 to 0.109375
- v_factors: bfloat16 [24, 24, 1024, 128], P('row', 'col'), may hold values from -0.1875 to 0.1875
- tile_scales: float32 [24, 24, 128], P('row', 'col'), may hold values from 0.3 to 3
- rank_class: int32 [24, 24], P('row', 'col'), may hold values from 0 to 3, as said below
- slopes: float32 [64, 24576], P(None, 'row'), may hold values from -40 to 40
Outputs:
- solution_field: float32 [64, 24576], P(None, 'col')
- residual: float32 [64, 24576], P(None, 'col')
Inputs may be any that keep to these rules, and one draw needn't show every extreme that they name: `rank_class`: class k gives a tile of rank 128 / 8 * 2**k; tiles of one device tend to share high or low classes.
All inputs are finite; a program needn't handle non-finite values.
Results may differ from a plain program's by a relative error of at most 0.017.
Values may be sent and summed in bfloat16 or wider, within the bound.
A program may use at most 64 MiB of HBM per device.

v0:
```python
import jax
import jax.numpy as jnp
from jax import lax
from jax.sharding import PartitionSpec as P

ITERS = 2
damping = 0.1
epsilon = 1e-06


def rank_weights(tile_scales, rank_class):
    max_rank = tile_scales.shape[-1]
    ranks = jnp.left_shift(jnp.int32(max_rank // 8), rank_class)
    columns = lax.broadcasted_iota(jnp.int32, tile_scales.shape, 2)
    return jnp.where(columns < ranks[:, :, None], tile_scales, jnp.zeros_like(tile_scales))


def padded_apply(source, first_factor, second_factor, weights, transpose):
    rows_here, cols_here, tile_size, max_rank = first_factor.shape
    frames = source.shape[0]
    if transpose:
        pieces = source.reshape(frames, rows_here, tile_size)
        projected = jnp.einsum(
            "fis,ijsr->fijr", pieces, first_factor, preferred_element_type=jnp.float32
        )
        scaled = (projected * weights[None]).astype(jnp.bfloat16)
        result = jnp.einsum(
            "fijr,ijmr->fjm", scaled, second_factor, preferred_element_type=jnp.float32
        )
        return result.reshape(frames, cols_here * tile_size)
    pieces = source.reshape(frames, cols_here, tile_size)
    projected = jnp.einsum(
        "fjm,ijmr->fijr", pieces, first_factor, preferred_element_type=jnp.float32
    )
    scaled = (projected * weights[None]).astype(jnp.bfloat16)
    result = jnp.einsum("fijr,ijsr->fis", scaled, second_factor, preferred_element_type=jnp.float32)
    return result.reshape(frames, rows_here * tile_size)


def apply_tiles(source, first_factor, second_factor, weights, transpose):
    return padded_apply(source, first_factor, second_factor, weights, transpose)


def per_device(u_factors, v_factors, tile_scales, rank_class, slopes):
    weights = rank_weights(tile_scales, rank_class)
    rows_here, cols_here, tile_size, max_rank = u_factors.shape
    share_width = cols_here * tile_size // lax.axis_size("row")
    offset = lax.axis_index("row") * share_width

    def backward(image_b):
        partial_value = apply_tiles(image_b, u_factors, v_factors, weights, True)
        return lax.psum(partial_value, "row")

    def own_part(field):
        return lax.dynamic_slice_in_dim(field, offset, share_width, 1)

    def frame_product(left_field, right_field):
        return jnp.sum(own_part(left_field) * own_part(right_field), axis=1)

    right_side = backward(slopes.astype(jnp.bfloat16))
    solution_field = jnp.zeros_like(right_side)
    residual = right_side
    direction = right_side
    norm_now = lax.psum(frame_product(residual, residual), ("row", "col"))
    dir_norm = norm_now
    for sweep in range(ITERS):
        narrowed = direction.astype(jnp.bfloat16)
        forward_partial_value = apply_tiles(narrowed, v_factors, u_factors, weights, False)
        forward_image = lax.psum(forward_partial_value, "col")
        image_norm = lax.psum(jnp.sum(forward_image * forward_image, axis=1), "row")
        dir_norm = lax.psum(frame_product(direction, direction), ("row", "col"))
        operator_image = backward(forward_image.astype(jnp.bfloat16)) + damping * direction
        step_size = norm_now / (image_norm + damping * dir_norm + epsilon)
        solution_field = solution_field + step_size[:, None] * direction
        residual = residual - step_size[:, None] * operator_image
        if sweep + 1 < ITERS:
            norm_next = lax.psum(frame_product(residual, residual), ("row", "col"))
            growth = norm_next / (norm_now + epsilon)
            direction = residual + growth[:, None] * direction
            norm_now = norm_next
    return (solution_field, residual)


def solution(mesh):
    return jax.shard_map(
        per_device,
        mesh=mesh,
        in_specs=(
            P("row", "col", None, None),
            P("row", "col", None, None),
            P("row", "col", None),
            P("row", "col"),
            P(None, "row"),
        ),
        out_specs=(P(None, "col"), P(None, "col")),
        check_vma=False,
    )
```

profile of v0, /device:TPU:0, one launch (start us, length us, event | category | flops | bytes accessed | tf_op | source)
XLA Modules:
  0.0 383.3 jit_solution(15641545947727971645)
XLA Ops:
  10.4 6.1 %fusion.12 = f32[6,8,8,1024]{3,2,1,0:T(8,128)S(1)} fusion(bf16[3,6,1024,128]{3,2,1,0:T(8,128)(2,1)} %param.6, bf16[3,6,1024,128]{3,2,1,0:T(8,128)(2,1)} %param.5, bf16[64,3,1024,1]{2,1,0,3:T(4,128)(2,1)S(1)} %reshape.49, f32[3,6,128]{2,0,1:T(4,128)S(1)} %copy.12), kind=kOutput, calls=%fused_computation.16 | convolution fusion | flops 604274688 | bytes 11412480 | tf_op jit(solution)/shard_map/fijr,ijmr->fjm/dot_general | solution.py:27
  17.9 61.8 %all-reduce.6.cloned.1.call-done = f32[64,6144]{1,0:T(8,128)} async-done(((f32[64,6144]{1,0:T(8,128)}), f32[64,6144]{1,0:T(8,128)}) %all-reduce.6.cloned.1.call-update) | async-done | bytes 1572880 | tf_op jit(solution)/shard_map/psum | solution.py:52
  79.7 1.5 convert_element_type.42
  82.2 6.6 %convolution_bitcast_fusion.1 = f32[3,8,8,1024]{3,2,1,0:T(8,128)S(1)} fusion(bf16[3,6,1024,128]{3,2,1,0:T(8,128)(2,1)} %param.5, bf16[3,6,1024,128]{3,2,1,0:T(8,128)(2,1)} %param.6, bf16[64,6,1024,1]{2,1,0,3:T(8,128)(2,1)S(1)} %reshape.51, f32[3,6,128]{2,1,0:T(8,128)S(1)} %fusion.73), kind=kOutput, calls=%fused_computation.20 | convolution fusion | flops 604274688 | bytes 11019264 | tf_op jit(solution)/shard_map/fijr,ijsr->fis/dot_general | solution.py:36
  89.7 43.1 %all-reduce.8.cloned.1.call-done = f32[64,3072]{1,0:T(8,128)} async-done(((f32[64,3072]{1,0:T(8,128)}), f32[64,3072]{1,0:T(8,128)}) %all-reduce.8.cloned.1.call-update) | async-done | bytes 786448 | tf_op jit(solution)/shard_map/psum | solution.py:69
  132.9 1.6 multiply_reduce_fusion.1
  135.0 6.1 %fusion.15 = f32[6,8,8,1024]{3,2,1,0:T(8,128)S(1)} fusion(bf16[3,6,1024,128]{3,2,1,0:T(8,128)(2,1)} %param.6, bf16[3,6,1024,128]{3,2,1,0:T(8,128)(2,1)} %param.5, bf16[64,3,1024,1]{2,1,0,3:T(4,128)(2,1)S(1)} %reshape.53, f32[3,6,128]{2,0,1:T(4,128)S(1)} %copy.12), kind=kOutput, calls=%fused_computation.17 | convolution fusion | flops 604274688 | bytes 11412480 | tf_op jit(solution)/shard_map/fijr,ijmr->fjm/dot_general | solution.py:27
  143.9 39.8 %psum.74 = f32[64]{0:T(128)S(1)} all-reduce(f32[64]{0:T(128)S(1)} %multiply_reduce_fusion.4), channel_id=1, replica_groups=mesh['row'=8,'col'=4] {'row','col'}, use_global_device_ids=true, to_apply=%region_2.3 | all-reduce | flops 64 | bytes 512 | tf_op jit(solution)/shard_map/psum | solution.py:64
  183.8 12.9 %psum.76 = f32[64]{0:T(128)S(1)} all-reduce(f32[64]{0:T(128)S(1)} %get-tuple-element.8), channel_id=1, replica_groups=mesh['row'=8,'col'=4] {'row'}, use_global_device_ids=true, to_apply=%region_5.6 | all-reduce | flops 64 | bytes 512 | tf_op jit(solution)/shard_map/psum | solution.py:70
  196.7 4.7 %all-reduce.10.cloned.1.call-done = f32[64,6144]{1,0:T(8,128)} async-done(((f32[64,6144]{1,0:T(8,128)}), f32[64,6144]{1,0:T(8,128)}) %all-reduce.10.cloned.1.call-update) | async-done | bytes 1572880 | tf_op jit(solution)/shard_map/psum | solution.py:52
  201.4 1.7 multiply_subtract_fusion.1
  203.2 39.7 %psum.78 = f32[64]{0:T(128)S(1)} all-reduce(f32[64]{0:T(128)S(1)} %multiply_reduce_fusion.3), channel_id=1, replica_groups=mesh['row'=8,'col'=4] {'row','col'}, use_global_device_ids=true, to_apply=%region_8.9 | all-reduce | flops 64 | bytes 512 | tf_op jit(solution)/shard_map/psum | solution.py:77
  242.8 1.7 fusion.74
  244.5 2.8 reshape.55
  247.3 7.7 %convolution_bitcast_fusion = f32[3,8,8,1024]{3,2,1,0:T(8,128)} fusion(bf16[3,6,1024,128]{3,2,1,0:T(8,128)(2,1)} %param.5, bf16[3,6,1024,128]{3,2,1,0:T(8,128)(2,1)} %param.6, bf16[64,6,1024,1]{2,1,0,3:T(8,128)(2,1)} %reshape.55, f32[3,6,128]{2,1,0:T(8,128)S(1)} %fusion.73), kind=kOutput, calls=%fused_computation.19 | convolution fusion | flops 604274688 | bytes 11019264 | tf_op jit(solution)/shard_map/fijr,ijsr->fis/dot_general | solution.py:36
  255.1 2.1 copy.36
  257.2 43.6 %all-reduce.12.cloned.1.call-done = f32[64,3072]{1,0:T(8,128)} async-done(((f32[64,3072]{1,0:T(8,128)}), f32[64,3072]{1,0:T(8,128)}) %all-reduce.12.cloned.1.call-update) | async-done | bytes 786448 | tf_op jit(solution)/shard_map/psum | solution.py:69
  300.8 2.1 fusion.75
  304.1 7.4 %fusion.18 = f32[6,8,8,1024]{3,2,1,0:T(8,128)} fusion(bf16[3,6,1024,128]{3,2,1,0:T(8,128)(2,1)} %param.6, bf16[3,6,1024,128]{3,2,1,0:T(8,128)(2,1)} %param.5, bf16[64,3,1024,1]{2,1,0,3:T(4,128)(2,1)} %reshape.57, f32[3,6,128]{2,0,1:T(4,128)S(1)} %copy.12), kind=kOutput, calls=%fused_computation.18 | convolution fusion | flops 604274688 | bytes 11412480 | tf_op jit(solution)/shard_map/fijr,ijmr->fjm/dot_general | solution.py:27
  311.5 2.7 copy.37
  315.3 40.0 %psum.81 = f32[64]{0:T(128)S(1)} all-reduce(f32[64]{0:T(128)S(1)} %multiply_reduce_fusion.2), channel_id=1, replica_groups=mesh['row'=8,'col'=4] {'row','col'}, use_global_device_ids=true, to_apply=%region_13.14 | all-reduce | flops 64 | bytes 512 | tf_op jit(solution)/shard_map/psum | solution.py:71
  355.3 12.9 %psum.80 = f32[64]{0:T(128)S(1)} all-reduce(f32[64]{0:T(128)S(1)} %copy-done.1), channel_id=1, replica_groups=mesh['row'=8,'col'=4] {'row'}, use_global_device_ids=true, to_apply=%region_11.12 | all-reduce | flops 64 | bytes 512 | tf_op jit(solution)/shard_map/psum | solution.py:70
  368.2 4.6 %all-reduce.14.cloned.1.call-done = f32[64,6144]{1,0:T(8,128)} async-done(((f32[64,6144]{1,0:T(8,128)}), f32[64,6144]{1,0:T(8,128)}) %all-reduce.14.cloned.1.call-update) | async-done | bytes 1572880 | tf_op jit(solution)/shard_map/psum | solution.py:52
  372.8 4.0 %multiply_subtract_fusion = (f32[64,6144]{1,0:T(8,128)}, f32[64,6144]{1,0:T(8,128)}) fusion(f32[64,6144]{1,0:T(8,128)S(1)} %multiply_subtract_fusion.1, f32[64,6144]{1,0:T(8,128)} %all-reduce.14.cloned.1.call-done, f32[64,6144]{1,0:T(8,128)} %get-tuple-element.3, f32[64]{0:T(128)S(1)} %add_divide_fusion, f32[64,6144]{1,0:T(8,128)S(1)} %copy-done, ...), kind=kLoop, calls=%fused_computation.12 | loop fusion | flops 2752512 | bytes 9437696 | tf_op jit(solution)/shard_map/sub | solution.py:75
  (35 shorter events, 12.5 us)
Async XLA Ops:
  7.2 72.5 %all-reduce.6.cloned.1.call-start = ((), (), s32[]{:S(2)}) async-start(), calls=%async_computation | async-start | bytes 3145728 | tf_op jit(solution)/shard_map/psum | solution.py:52
  17.9 115.0 %all-reduce.8.cloned.1.call-start = ((), (), s32[]{:S(2)}) async-start(), calls=%async_computation.1 | async-start | bytes 1572864 | tf_op jit(solution)/shard_map/psum | solution.py:69
  89.7 111.7 %all-reduce.10.cloned.1.call-start = ((), (), s32[]{:S(2)}) async-start(), calls=%async_computation.2 | async-start | bytes 3145728 | tf_op jit(solution)/shard_map/psum | solution.py:52
  142.4 1.4 copy-start
  142.4 158.4 %all-reduce.12.cloned.1.call-start = ((), (), s32[]{:S(2)}) async-start(), calls=%async_computation.3 | async-start | bytes 1572864 | tf_op jit(solution)/shard_map/psum | solution.py:69
  242.8 1.7 copy-start.2
  257.2 115.6 %all-reduce.14.cloned.1.call-start = ((), (), s32[]{:S(2)}) async-start(), calls=%async_computation.4 | async-start | bytes 3145728 | tf_op jit(solution)/shard_map/psum | solution.py:52
  314.2 41.0 %copy-start.1 = (f32[64]{0:T(128)S(1)}, f32[64]{0:T(128)}, u32[]{:S(2)}) copy-start(f32[64]{0:T(128)} %get-tuple-element.7) | copy-start | bytes 772
  314.2 54.0 %copy-start.3 = (f32[64]{0:T(128)S(1)}, f32[64]{0:T(128)}, u32[]{:S(2)}) copy-start(f32[64]{0:T(128)} %copy-done.2) | copy-start | bytes 772
Sparse Core Ops, SparseCore 0:
  18.0 61.6 all-reduce.5
  89.8 43.0 all-reduce.7
  142.6 58.7 all-reduce.9
  257.3 43.4 all-reduce.11
  314.4 58.3 all-reduce.13
where the time goes:
time: 384 us; the launch traced here: 383 us
  waiting for transfers between devices  158 us (41%)
  blocking collectives  145 us (38%)
  matrix products  33.8 us (9%)
  other arithmetic  16.4 us (4%)
  local copies, waits for them, and re-layouts  15.9 us (4%)
  between operations  13.9 us (4%)
    psum x2, waiting for transfers between devices, per_device(): forward_image = lax.psum(forward_partial_value, 'col')  86.7 us
    psum x3, waiting for transfers between devices, backward(): return lax.psum(partial_value, 'row')  71 us
    psum x1, blocking collectives, per_device(): dir_norm = lax.psum(frame_product(direction, direction), ('row', 'col'))  40 us
    psum x1, blocking collectives, per_device(): norm_now = lax.psum(frame_product(residual, residual), ('row', 'col'))  39.8 us
    psum x1, blocking collectives, per_device(): norm_next = lax.psum(frame_product(residual, residual), ('row', 'col'))  39.7 us
    psum x2, blocking collectives, per_device(): image_norm = lax.psum(jnp.sum(forward_image * forward_image, axis=1), 'row')  25.8 us
    dot_general x3, matrix products, padded_apply(): jnp.einsum('fijr,ijmr->fjm', scaled, second_factor, preferred_element_typ...  19.5 us
    dot_general x2, matrix products, padded_apply(): jnp.einsum('fijr,ijsr->fis', scaled, second_factor, preferred_element_typ...  14.3 us
  transfers between devices with their start and end apart: 5, of which 5 were waited for; matrix products, arithmetic and copies ran while one was open for 0% of the time, Pallas kernels for 0%

commit v1 on v0

--- a/solution.py
+++ b/solution.py
@@ -66,7 +66,11 @@
     for sweep in range(ITERS):
         narrowed = direction.astype(jnp.bfloat16)
         forward_partial_value = apply_tiles(narrowed, v_factors, u_factors, weights, False)
-        forward_image = lax.psum(forward_partial_value, "col")
+        forward_image = forward_partial_value
+        for hop in (1, 2):
+            forward_image = forward_image + lax.ppermute(
+                forward_image, "col", [(dev, dev ^ hop) for dev in range(4)]
+            )
         image_norm = lax.psum(jnp.sum(forward_image * forward_image, axis=1), "row")
         dir_norm = lax.psum(frame_product(direction, direction), ("row", "col"))
         operator_image = backward(forward_image.astype(jnp.bfloat16)) + damping * direction

time: 384 us -> 401 us (1.044)
  waiting for transfers between devices: 158 us -> 174 us
  starting transfers between devices: 0.21 us -> 8.26 us
    ppermute x0 -> x4, waiting for transfers between devices: none -> 99.3 us  [per_device(): lax.ppermute(forward_image, 'col', [(dev, dev ^ hop) for dev in range(4)])]
    psum x2 -> x0, waiting for transfers between devices: 86.7 us -> none  [per_device(): forward_image = lax.psum(forward_partial_value, 'col')]
    ppermute x0 -> x4, starting transfers between devices: none -> 8.14 us  [per_device(): lax.ppermute(forward_image, 'col', [(dev, dev ^ hop) for dev in range(4)])]
  transfers between devices with their start and end apart: 5 -> 7, of which waited for: 5 -> 7; matrix products, arithmetic and copies ran while one was open for 0% -> 0% of each run, Pallas kernels for 0% -> 0%
where the time goes in v1:
time: 401 us; the launch traced here: 400 us
  waiting for transfers between devices  174 us (43%)
  blocking collectives  142 us (35%)
  matrix products  33.8 us (8%)
  local copies, waits for them, and re-layouts  14.2 us (4%)
  other arithmetic  13.9 us (3%)
  between operations  13.8 us (3%)
  starting transfers between devices  8.26 us (2%)
    ppermute x4, waiting for transfers between devices, per_device(): lax.ppermute(forward_image, 'col', [(dev, dev ^ hop) for dev in range(4)])  99.3 us
    psum x3, waiting for transfers between devices, backward(): return lax.psum(partial_value, 'row')  74.6 us
    psum x1, blocking collectives, per_device(): norm_next = lax.psum(frame_product(residual, residual), ('row', 'col'))  39.7 us
    psum x1, blocking collectives, per_device(): norm_now = lax.psum(frame_product(residual, residual), ('row', 'col'))  38.6 us
    psum x1, blocking collectives, per_device(): dir_norm = lax.psum(frame_product(direction, direction), ('row', 'col'))  38.4 us
    psum x2, blocking collectives, per_device(): image_norm = lax.psum(jnp.sum(forward_image * forward_image, axis=1), 'row')  25.6 us
    dot_general x3, matrix products, padded_apply(): jnp.einsum('fijr,ijmr->fjm', scaled, second_factor, preferred_element_typ...  19.6 us
    dot_general x2, matrix products, padded_apply(): jnp.einsum('fijr,ijsr->fis', scaled, second_factor, preferred_element_typ...  14.3 us
  transfers between devices with their start and end apart: 7, of which 7 were waited for; matrix products, arithmetic and copies ran while one was open for 0% of the time, Pallas kernels for 0%

profile of v1, /device:TPU:0, one launch (start us, length us, event | category | flops | bytes accessed | tf_op | source)
XLA Modules:
  0.0 400.2 jit_solution(4874403974233068478)
XLA Ops:
  10.4 6.1 %fusion.12 = f32[6,8,8,1024]{3,2,1,0:T(8,128)S(1)} fusion(bf16[3,6,1024,128]{3,2,1,0:T(8,128)(2,1)} %param.6, bf16[3,6,1024,128]{3,2,1,0:T(8,128)(2,1)} %param.5, bf16[64,3,1024,1]{2,1,0,3:T(4,128)(2,1)S(1)} %reshape.49, f32[3,6,128]{2,0,1:T(4,128)S(1)} %copy.12), kind=kOutput, calls=%fused_computation.16 | convolution fusion | flops 604274688 | bytes 11412480 | tf_op jit(solution)/shard_map/fijr,ijmr->fjm/dot_general | solution.py:27
  17.9 61.8 %all-reduce.4.cloned.1.call-done = f32[64,6144]{1,0:T(8,128)} async-done(((f32[64,6144]{1,0:T(8,128)}), f32[64,6144]{1,0:T(8,128)}) %all-reduce.4.cloned.1.call-update) | async-done | bytes 1572880 | tf_op jit(solution)/shard_map/psum | solution.py:52
  82.2 6.6 %convolution_bitcast_fusion.1 = f32[3,8,8,1024]{3,2,1,0:T(8,128)S(1)} fusion(bf16[3,6,1024,128]{3,2,1,0:T(8,128)(2,1)} %param.5, bf16[3,6,1024,128]{3,2,1,0:T(8,128)(2,1)} %param.6, bf16[64,6,1024,1]{2,1,0,3:T(8,128)(2,1)S(1)} %reshape.51, f32[3,6,128]{2,1,0:T(8,128)S(1)} %fusion.73), kind=kOutput, calls=%fused_computation.20 | convolution fusion | flops 604274688 | bytes 11019264 | tf_op jit(solution)/shard_map/fijr,ijsr->fis/dot_general | solution.py:36
  88.8 1.7 collective-permute-start
  90.5 16.7 %collective-permute-done = f32[64,3072]{1,0:T(8,128)S(1)} collective-permute-done((f32[64,3072]{1,0:T(8,128)S(1)}, f32[64,3072]{1,0:T(8,128)S(1)}, u32[]{:S(2)}, u32[]{:S(2)}) %collective-permute-start) | collective-permute-done | bytes 786464 | tf_op jit(solution)/shard_map/ppermute | solution.py:71
  107.2 2.5 collective-permute-start.1
  109.7 32.7 %collective-permute-done.1 = f32[64,3072]{1,0:T(8,128)S(1)} collective-permute-done((f32[64,3072]{1,0:T(8,128)S(1)}, f32[64,3072]{1,0:T(8,128)S(1)}, u32[]{:S(2)}, u32[]{:S(2)}) %collective-permute-start.1) | collective-permute-done | bytes 786464 | tf_op jit(solution)/shard_map/ppermute | solution.py:71
  143.2 6.1 %fusion.15 = f32[6,8,8,1024]{3,2,1,0:T(8,128)S(1)} fusion(bf16[3,6,1024,128]{3,2,1,0:T(8,128)(2,1)} %param.6, bf16[3,6,1024,128]{3,2,1,0:T(8,128)(2,1)} %param.5, bf16[64,3,1024,1]{2,1,0,3:T(4,128)(2,1)S(1)} %reshape.53, f32[3,6,128]{2,0,1:T(4,128)S(1)} %copy.12), kind=kOutput, calls=%fused_computation.17 | convolution fusion | flops 604274688 | bytes 11412480 | tf_op jit(solution)/shard_map/fijr,ijmr->fjm/dot_general | solution.py:27
  152.1 38.6 %psum.60 = f32[64]{0:T(128)S(1)} all-reduce(f32[64]{0:T(128)S(1)} %multiply_reduce_fusion.4), channel_id=1, replica_groups=mesh['row'=8,'col'=4] {'row','col'}, use_global_device_ids=true, to_apply=%region_2.3 | all-reduce | flops 64 | bytes 512 | tf_op jit(solution)/shard_map/psum | solution.py:64
  190.7 12.8 %psum.61 = f32[64]{0:T(128)S(1)} all-reduce(f32[64]{0:T(128)S(1)} %get-tuple-element.8), channel_id=1, replica_groups=mesh['row'=8,'col'=4] {'row'}, use_global_device_ids=true, to_apply=%region_4.5 | all-reduce | flops 64 | bytes 512 | tf_op jit(solution)/shard_map/psum | solution.py:74
  203.5 6.2 %all-reduce.6.cloned.1.call-done = f32[64,6144]{1,0:T(8,128)} async-done(((f32[64,6144]{1,0:T(8,128)}), f32[64,6144]{1,0:T(8,128)}) %all-reduce.6.cloned.1.call-update) | async-done | bytes 1572880 | tf_op jit(solution)/shard_map/psum | solution.py:52
  211.5 39.7 %psum.63 = f32[64]{0:T(128)S(1)} all-reduce(f32[64]{0:T(128)S(1)} %multiply_reduce_fusion.3), channel_id=1, replica_groups=mesh['row'=8,'col'=4] {'row','col'}, use_global_device_ids=true, to_apply=%region_7.8 | all-reduce | flops 64 | bytes 512 | tf_op jit(solution)/shard_map/psum | solution.py:81
  251.2 1.7 fusion.74
  252.9 2.8 reshape.55
  255.7 7.7 %convolution_bitcast_fusion = f32[3,8,8,1024]{3,2,1,0:T(8,128)} fusion(bf16[3,6,1024,128]{3,2,1,0:T(8,128)(2,1)} %param.5, bf16[3,6,1024,128]{3,2,1,0:T(8,128)(2,1)} %param.6, bf16[64,6,1024,1]{2,1,0,3:T(8,128)(2,1)} %reshape.55, f32[3,6,128]{2,1,0:T(8,128)S(1)} %fusion.73), kind=kOutput, calls=%fused_computation.19 | convolution fusion | flops 604274688 | bytes 11019264 | tf_op jit(solution)/shard_map/fijr,ijsr->fis/dot_general | solution.py:36
  266.2 17.0 %collective-permute-done.2 = f32[64,3072]{1,0:T(8,128)S(1)} collective-permute-done((f32[64,3072]{1,0:T(8,128)S(1)}, f32[64,3072]{1,0:T(8,128)S(1)}, u32[]{:S(2)}, u32[]{:S(2)}) %collective-permute-start.2) | collective-permute-done | bytes 786464 | tf_op jit(solution)/shard_map/ppermute | solution.py:71
  283.3 2.4 collective-permute-start.3
  285.7 33.0 %collective-permute-done.3 = f32[64,3072]{1,0:T(8,128)S(1)} collective-permute-done((f32[64,3072]{1,0:T(8,128)S(1)}, f32[64,3072]{1,0:T(8,128)S(1)}, u32[]{:S(2)}, u32[]{:S(2)}) %collective-permute-start.3) | collective-permute-done | bytes 786464 | tf_op jit(solution)/shard_map/ppermute | solution.py:71
  320.6 7.4 %fusion.18 = f32[6,8,8,1024]{3,2,1,0:T(8,128)} fusion(bf16[3,6,1024,128]{3,2,1,0:T(8,128)(2,1)} %param.6, bf16[3,6,1024,128]{3,2,1,0:T(8,128)(2,1)} %param.5, bf16[64,3,1024,1]{2,1,0,3:T(4,128)(2,1)} %reshape.57, f32[3,6,128]{2,0,1:T(4,128)S(1)} %copy.12), kind=kOutput, calls=%fused_computation.18 | convolution fusion | flops 604274688 | bytes 11412480 | tf_op jit(solution)/shard_map/fijr,ijmr->fjm/dot_general | solution.py:27
  328.0 2.7 copy.37
  331.8 38.4 %psum.65 = f32[64]{0:T(128)S(1)} all-reduce(f32[64]{0:T(128)S(1)} %multiply_reduce_fusion.2), channel_id=1, replica_groups=mesh['row'=8,'col'=4] {'row','col'}, use_global_device_ids=true, to_apply=%region_11.12 | all-reduce | flops 64 | bytes 512 | tf_op jit(solution)/shard_map/psum | solution.py:75
  370.2 12.8 %psum.64 = f32[64]{0:T(128)S(1)} all-reduce(f32[64]{0:T(128)S(1)} %copy-done.1), channel_id=1, replica_groups=mesh['row'=8,'col'=4] {'row'}, use_global_device_ids=true, to_apply=%region_9.10 | all-reduce | flops 64 | bytes 512 | tf_op jit(solution)/shard_map/psum | solution.py:74
  383.0 6.6 %all-reduce.8.cloned.1.call-done = f32[64,6144]{1,0:T(8,128)} async-done(((f32[64,6144]{1,0:T(8,128)}), f32[64,6144]{1,0:T(8,128)}) %all-reduce.8.cloned.1.call-update) | async-done | bytes 1572880 | tf_op jit(solution)/shard_map/psum | solution.py:52
  389.7 4.0 %multiply_subtract_fusion = (f32[64,6144]{1,0:T(8,128)}, f32[64,6144]{1,0:T(8,128)}) fusion(f32[64,6144]{1,0:T(8,128)S(1)} %multiply_subtract_fusion.1, f32[64,6144]{1,0:T(8,128)} %all-reduce.8.cloned.1.call-done, f32[64,6144]{1,0:T(8,128)} %get-tuple-element.3, f32[64]{0:T(128)S(1)} %add_divide_fusion, f32[64,6144]{1,0:T(8,128)S(1)} %copy-done, ...), kind=kLoop, calls=%fused_computation.12 | loop fusion | flops 2752512 | bytes 9437696 | tf_op jit(solution)/shard_map/sub | solution.py:79
  (39 shorter events, 18.5 us)
Async XLA Ops:
  7.2 72.5 %all-reduce.4.cloned.1.call-start = ((), (), s32[]{:S(2)}) async-start(), calls=%async_computation | async-start | bytes 3145728 | tf_op jit(solution)/shard_map/psum | solution.py:52
  17.9 191.8 %all-reduce.6.cloned.1.call-start = ((), (), s32[]{:S(2)}) async-start(), calls=%async_computation.1 | async-start | bytes 3145728 | tf_op jit(solution)/shard_map/psum | solution.py:52
  88.8 18.4 %collective-permute-start = (f32[64,3072]{1,0:T(8,128)S(1)}, f32[64,3072]{1,0:T(8,128)S(1)}, u32[]{:S(2)}, u32[]{:S(2)}) collective-permute-start(f32[64,3072]{1,0:T(8,128)S(1)} %bitcast.70), channel_id=1, source_target_pairs={{0,1},{1,0},{2,3},{3,2},{4,5},{5,4},{6,7},{7,6},{8,9},{9,8},{10,11... | collective-permute-start | bytes 2359304 | tf_op jit(solution)/shard_map/ppermute | solution.py:71
  107.2 35.2 %collective-permute-start.1 = (f32[64,3072]{1,0:T(8,128)S(1)}, f32[64,3072]{1,0:T(8,128)S(1)}, u32[]{:S(2)}, u32[]{:S(2)}) collective-permute-start(f32[64,3072]{1,0:T(8,128)S(1)} %add.67), channel_id=1, source_target_pairs={{0,2},{1,3},{2,0},{3,1},{4,6},{5,7},{6,4},{7,5},{8,10},{9,11},{10,... | collective-permute-start | bytes 2359304 | tf_op jit(solution)/shard_map/ppermute | solution.py:71
  150.6 1.4 copy-start
  150.6 239.1 %all-reduce.8.cloned.1.call-start = ((), (), s32[]{:S(2)}) async-start(), calls=%async_computation.2 | async-start | bytes 3145728 | tf_op jit(solution)/shard_map/psum | solution.py:52
  251.2 1.7 copy-start.2
  264.7 18.5 %collective-permute-start.2 = (f32[64,3072]{1,0:T(8,128)S(1)}, f32[64,3072]{1,0:T(8,128)S(1)}, u32[]{:S(2)}, u32[]{:S(2)}) collective-permute-start(f32[64,3072]{1,0:T(8,128)S(1)} %bitcast.72), channel_id=1, source_target_pairs={{0,1},{1,0},{2,3},{3,2},{4,5},{5,4},{6,7},{7,6},{8,9},{9,8},{10,11... | collective-permute-start | bytes 2359304 | tf_op jit(solution)/shard_map/ppermute | solution.py:71
  283.3 35.4 %collective-permute-start.3 = (f32[64,3072]{1,0:T(8,128)S(1)}, f32[64,3072]{1,0:T(8,128)S(1)}, u32[]{:S(2)}, u32[]{:S(2)}) collective-permute-start(f32[64,3072]{1,0:T(8,128)S(1)} %add.74), channel_id=1, source_target_pairs={{0,2},{1,3},{2,0},{3,1},{4,6},{5,7},{6,4},{7,5},{8,10},{9,11},{10,... | collective-permute-start | bytes 2359304 | tf_op jit(solution)/shard_map/ppermute | solution.py:71
  330.7 39.5 %copy-start.1 = (f32[64]{0:T(128)S(1)}, f32[64]{0:T(128)}, u32[]{:S(2)}) copy-start(f32[64]{0:T(128)} %get-tuple-element.7) | copy-start | bytes 772
  330.7 52.3 %copy-start.3 = (f32[64]{0:T(128)S(1)}, f32[64]{0:T(128)}, u32[]{:S(2)}) copy-start(f32[64]{0:T(128)} %copy-done.2) | copy-start | bytes 772
Sparse Core Ops, SparseCore 0:
  18.0 61.6 all-reduce.3
  150.7 58.9 all-reduce.5
  330.9 58.7 all-reduce.7
